TPU v7x, 32 devices: a whole 2x2x4 slice. The times are simulated.
32 devices in a mesh: seq: 2 (over x), rows: 4 (over z), col: 4 (over y, core).
Axes of the slice: x: 2, y: 2, z: 4, core: 2. Of those that a mesh axis runs over, the one named last changes fastest.
Arguments:
- tokens: bfloat16 [16, 512, 768], P(('rows', 'col'), 'seq'), may hold values from -6 to 6
- lengths: int32 [16, 4], P(('rows', 'col')), may hold values from 1 to 320, 512 in all within a row
- qkv_weight: bfloat16 [2, 3, 768, 768], replicated, may hold values from -0.21875 to 0.21875
- out_weight: bfloat16 [2, 768, 768], replicated, may hold values from -0.875 to 0.875
- rel_table: bfloat16 [2, 512, 768], replicated, may hold values from -5 to 5
- ffn_in: bfloat16 [2, 768, 3072], P(None, None, 'col'), may hold values from -0.21875 to 0.21875
- ffn_out: bfloat16 [2, 768, 3072], P(None, None, 'col'), may hold values from -0.109375 to 0.109375
- norm_params: float32 [2, 4, 768], replicated, may hold values from -0.8 to 1.4, as said below
- cotangent: bfloat16 [16, 512, 768], P(('rows', 'col'), 'seq'), may hold values from -6 to 6
Outputs:
- output: float32 [16, 512, 768], P(('rows', 'col'), 'seq')
- input_grad: float32 [16, 512, 768], P(('rows', 'col'), 'seq')
- grad_qkv: float32 [2, 3, 768, 768], P(None, None, ('seq', 'rows'), 'col')
- grad_out: float32 [2, 768, 768], P(None, ('seq', 'rows'), 'col')
- grad_rel: float32 [2, 512, 768], P(None, ('seq', 'rows'), 'col')
- grad_ffn_in: float32 [2, 768, 3072], P(None, ('seq', 'rows'), 'col')
- grad_ffn_out: float32 [2, 768, 3072], P(None, ('seq', 'rows'), 'col')
- grad_norms: float32 [2, 4, 768], P(None, 'col', ('seq', 'rows'))
Inputs may be any that keep to these rules, and one draw needn't show every extreme that they name: Each row's 4 document lengths sum to 512, and the longest of each row has exactly 320 tokens. `norm_params`: rows 0 and 2 of each layer are gains, rows 1 and 3 biases.
All inputs are finite; a program needn't handle non-finite values.
Results may differ from a plain program's by a relative error of at most 0.03.
Values may be sent and summed in bfloat16 or wider, within the bound.
No kernel may reach another device: no remote copies, remote signals or barrier semaphores. Data moves between devices by JAX's collectives and lax.ppermute only.
A program may use at most 256 MiB of HBM per device.

v0:
```python
import jax
import jax.numpy as jnp
import numpy as np
from jax import lax
from jax.sharding import PartitionSpec as P

HEADS = 12
HEAD_DIM = 64
SPAN = 256
MAX_REL = 512


NEGATIVE = -1000000000.0
EPSILON = 1e-07
HIGHEST = lax.Precision.HIGHEST


def offset_table(length, span_size, max_relative):
    relative = length - 1 - np.arange(2 * length)
    middle = span_size // 2
    absolute = np.where((relative < middle) & (relative > -middle), middle - 1, np.abs(relative))
    absolute = np.maximum(absolute, 1)
    log_position = (
        np.ceil(np.log(absolute / middle) / np.log((max_relative - 1) / middle) * (middle - 1))
        + middle
    )
    bucket = np.where(absolute <= middle, relative, log_position * np.sign(relative))
    bucket = np.clip(bucket + span_size, 0, 2 * span_size - 1)
    table = (bucket[:, None] == np.arange(2 * span_size)[None, :]) & (
        np.arange(2 * length) < 2 * length - 1
    )[:, None]
    return table.astype(np.float32)


def layer_norm(stream, gain_row, bias_row):
    row_mean = jnp.mean(stream, axis=-1, keepdims=True)
    centered = stream - row_mean
    row_var = jnp.mean(centered * centered, axis=-1, keepdims=True)
    return centered * lax.rsqrt(row_var + EPSILON) * gain_row + bias_row


def norm_back(state, gain_row, bias_row, d_result):
    unused_out, pull_back = jax.vjp(layer_norm, state, gain_row, bias_row)
    return pull_back(d_result)


def gelu_slope(hidden):
    cumulative = 0.5 * (1.0 + lax.erf(hidden * 0.7071067811865476))
    density = jnp.exp(-0.5 * hidden * hidden) * 0.3989422804014327
    return cumulative + hidden * density


def split_product(form, wide, narrow):
    upper = wide.astype(jnp.bfloat16)
    lower = (wide - upper.astype(jnp.float32)).astype(jnp.bfloat16)
    first = jnp.einsum(form, upper, narrow, preferred_element_type=jnp.float32)
    return first + jnp.einsum(form, lower, narrow, preferred_element_type=jnp.float32)


def skew_rows(source, shift, length):
    lead = source.shape[:-2]
    count, width = source.shape[-2:]
    flat = source.reshape(lead + (count * width,))
    flat = jnp.pad(flat, [(0, 0)] * len(lead) + [(0, width)])
    part = lax.dynamic_slice_in_dim(flat, shift, count * (width - 1), len(lead))
    return part.reshape(lead + (count, width - 1))[..., :length]


def relative_parts(query_heads, key_heads, pos_offsets, context):
    same_doc, offset = context
    total_len = key_heads.shape[1]
    local_len = query_heads.shape[1]
    query_shift = total_len - 1 - offset
    key_shift = total_len - 1 + offset
    query_rel = jnp.einsum(
        "rihe,mhe->rhim", query_heads, pos_offsets[1], preferred_element_type=jnp.float32
    )
    key_rel = jnp.einsum(
        "rjhe,mhe->rhjm", key_heads, pos_offsets[0], preferred_element_type=jnp.float32
    )

    def query_side(values):
        return skew_rows(values, query_shift, total_len)

    def key_side(values):
        return jnp.swapaxes(skew_rows(values, key_shift, local_len), 2, 3)

    return (query_rel, key_rel, query_side, key_side)


def score_rows(query_heads, key_heads, pos_offsets, context):
    same_doc = context[0]
    score_scale = (3.0 * HEAD_DIM) ** (-0.5)
    content = jnp.einsum(
        "rihe,rjhe->rhij", query_heads, key_heads, preferred_element_type=jnp.float32
    )
    query_rel, key_rel, query_side, key_side = relative_parts(
        query_heads, key_heads, pos_offsets, context
    )
    total = content + query_side(query_rel) + key_side(key_rel)
    return (
        jnp.where(same_doc, total * score_scale, NEGATIVE),
        (query_rel, key_rel, query_side, key_side),
    )


def attention_forward(stream, qkv, w_out, rel, norm_rows, context, table):
    row_count, local_len, model_width = stream.shape
    flat_in = stream.astype(jnp.bfloat16)
    projected = jnp.einsum(
        "rld,cde->crle", flat_in, qkv, preferred_element_type=jnp.float32
    ).astype(jnp.bfloat16)
    queries = projected[0]
    keys_all, values_all = (
        lax.all_gather(projected[1], "seq", axis=1, tiled=True),
        lax.all_gather(projected[2], "seq", axis=1, tiled=True),
    )
    total_len = keys_all.shape[1]
    pos_pair = jnp.einsum("bd,cde->cbe", rel, qkv[:2], preferred_element_type=jnp.float32).astype(
        jnp.bfloat16
    )
    pos_offsets = jnp.einsum(
        "mb,cbe->cme", table.astype(jnp.bfloat16), pos_pair, preferred_element_type=jnp.float32
    ).astype(jnp.bfloat16)
    pos_offsets = pos_offsets.reshape(2, table.shape[0], HEADS, HEAD_DIM)
    query_heads = queries.reshape(row_count, local_len, HEADS, HEAD_DIM)
    key_heads = keys_all.reshape(row_count, total_len, HEADS, HEAD_DIM)
    value_heads = values_all.reshape(row_count, total_len, HEADS, HEAD_DIM)
    scores, unused_parts = score_rows(query_heads, key_heads, pos_offsets, context)
    log_total = jax.nn.logsumexp(scores, axis=-1, keepdims=True)
    soft_rows = jnp.exp(scores - log_total).astype(jnp.bfloat16)
    attended = jnp.einsum(
        "rhij,rjhe->rihe", soft_rows, value_heads, preferred_element_type=jnp.float32
    )
    attended = attended.reshape(row_count, local_len, model_width).astype(jnp.bfloat16)
    branch = jnp.einsum("rld,de->rle", attended, w_out, preferred_element_type=jnp.float32)
    residual = stream + branch
    middle_state = layer_norm(residual, norm_rows[0], norm_rows[1])
    kept = (flat_in, queries, keys_all, values_all, pos_offsets, log_total, attended, residual)
    return (middle_state, kept)


def attention_backward(d_resid, kept, qkv, w_out, rel, context, table):
    flat_in, queries, keys_all, values_all, pos_offsets, log_total, attended, residual = kept
    row_count, local_len, model_width = flat_in.shape
    total_len = keys_all.shape[1]
    score_scale = (3.0 * HEAD_DIM) ** (-0.5)
    query_heads = queries.reshape(row_count, local_len, HEADS, HEAD_DIM)
    key_heads = keys_all.reshape(row_count, total_len, HEADS, HEAD_DIM)
    value_heads = values_all.reshape(row_count, total_len, HEADS, HEAD_DIM)
    d_branch = d_resid.astype(jnp.bfloat16)
    grad_out = jnp.einsum("rld,rle->de", attended, d_branch, preferred_element_type=jnp.float32)
    d_attended = jnp.einsum(
        "rle,de->rld", d_branch, w_out, preferred_element_type=jnp.float32
    ).astype(jnp.bfloat16)
    d_attended = d_attended.reshape(row_count, local_len, HEADS, HEAD_DIM)
    scores, parts = score_rows(query_heads, key_heads, pos_offsets, context)
    query_rel, key_rel, query_side, key_side = parts
    soft_full = jnp.exp(scores - log_total)
    d_values = jnp.einsum(
        "rhij,rihe->rjhe",
        soft_full.astype(jnp.bfloat16),
        d_attended,
        preferred_element_type=jnp.float32,
    )
    d_soft = jnp.einsum(
        "rihe,rjhe->rhij", d_attended, value_heads, preferred_element_type=jnp.float32
    )
    d_scores = (soft_full * (d_soft - jnp.sum(soft_full * d_soft, axis=-1, keepdims=True))).astype(
        jnp.bfloat16
    )
    d_queries = jnp.einsum(
        "rhij,rjhe->rihe", d_scores, key_heads, preferred_element_type=jnp.float32
    )
    d_keys = jnp.einsum(
        "rhij,rihe->rjhe", d_scores, query_heads, preferred_element_type=jnp.float32
    )
    score_grads = d_scores.astype(jnp.float32)
    unused_q, query_pull = jax.vjp(query_side, query_rel)
    unused_k, key_pull = jax.vjp(key_side, key_rel)
    d_query_rel = query_pull(score_grads)[0].astype(jnp.bfloat16)
    d_key_rel = key_pull(score_grads)[0].astype(jnp.bfloat16)
    d_queries = (
        d_queries
        + jnp.einsum(
            "rhim,mhe->rihe", d_query_rel, pos_offsets[1], preferred_element_type=jnp.float32
        )
    ) * score_scale
    d_keys = (
        d_keys
        + jnp.einsum(
            "rhjm,mhe->rjhe", d_key_rel, pos_offsets[0], preferred_element_type=jnp.float32
        )
    ) * score_scale
    d_key_offsets = jnp.einsum(
        "rhim,rihe->mhe", d_query_rel, query_heads, preferred_element_type=jnp.float32
    )
    d_query_offsets = jnp.einsum(
        "rhjm,rjhe->mhe", d_key_rel, key_heads, preferred_element_type=jnp.float32
    )
    d_pos_key = (
        jnp.dot(table.T, d_key_offsets.reshape(table.shape[0], model_width), precision=HIGHEST)
        * score_scale
    )
    d_pos_query = (
        jnp.dot(table.T, d_query_offsets.reshape(table.shape[0], model_width), precision=HIGHEST)
        * score_scale
    )
    d_keys, d_values = (
        lax.psum_scatter(
            d_keys.reshape(row_count, total_len, model_width).astype(jnp.bfloat16),
            "seq",
            scatter_dimension=1,
            tiled=True,
        ).astype(jnp.float32),
        lax.psum_scatter(
            d_values.reshape(row_count, total_len, model_width).astype(jnp.bfloat16),
            "seq",
            scatter_dimension=1,
            tiled=True,
        ).astype(jnp.float32),
    )
    stacked = jnp.stack(
        [d_queries.reshape(row_count, local_len, model_width), d_keys, d_values]
    ).astype(jnp.bfloat16)
    grad_qkv = jnp.einsum("rld,crle->cde", flat_in, stacked, preferred_element_type=jnp.float32)
    d_stream = d_resid + jnp.einsum(
        "crle,cde->rld", stacked, qkv, preferred_element_type=jnp.float32
    )
    d_pos = jnp.stack([d_pos_query, d_pos_key])
    pos_grad = split_product("cbe,bd->cde", d_pos, rel)
    grad_qkv = jnp.concatenate([grad_qkv[:2] + pos_grad, grad_qkv[2:]], axis=0)
    grad_rel = split_product("cbe,cde->bd", d_pos, qkv[:2])
    return (d_stream, grad_qkv, grad_out, grad_rel)


def ffn_forward(middle_state, w_in, w_down):
    row_count, local_len, model_width = middle_state.shape
    ffn_rows = middle_state.astype(jnp.bfloat16).reshape(row_count * local_len, model_width)
    gathered = lax.all_gather(ffn_rows, "col", axis=0, tiled=True)
    hidden = jnp.dot(gathered, w_in, preferred_element_type=jnp.float32)
    activated = jax.nn.gelu(hidden, approximate=False).astype(jnp.bfloat16)
    ffn_branch = lax.psum_scatter(
        jnp.einsum("tf,df->td", activated, w_down, preferred_element_type=jnp.float32).astype(
            jnp.bfloat16
        ),
        "col",
        scatter_dimension=0,
        tiled=True,
    ).astype(jnp.float32)
    kept = (gathered, w_in, w_down)
    return (ffn_branch.reshape(row_count, local_len, model_width), kept)


def ffn_backward(d_branch, kept):
    row_count, local_len, model_width = d_branch.shape
    d_rows = d_branch.reshape(row_count * local_len, model_width)
    source_rows, full_in, full_down = kept
    cot_rows = lax.all_gather(d_rows, "col", axis=0, tiled=True)
    hidden = jnp.dot(source_rows, full_in, preferred_element_type=jnp.float32)
    activated = jax.nn.gelu(hidden, approximate=False).astype(jnp.bfloat16)
    d_hidden = (
        jnp.dot(cot_rows, full_down, preferred_element_type=jnp.float32) * gelu_slope(hidden)
    ).astype(jnp.bfloat16)
    grad_down = jnp.einsum("td,tf->df", cot_rows, activated, preferred_element_type=jnp.float32)
    grad_in = jnp.einsum("td,tf->df", source_rows, d_hidden, preferred_element_type=jnp.float32)
    d_middle = lax.psum_scatter(
        jnp.einsum("tf,df->td", d_hidden, full_in, preferred_element_type=jnp.float32).astype(
            jnp.bfloat16
        ),
        "col",
        scatter_dimension=0,
        tiled=True,
    ).astype(jnp.float32)
    return (d_middle.reshape(row_count, local_len, model_width), grad_in, grad_down)


def per_device(
    tokens, lengths, qkv_weight, out_weight, rel_table, ffn_in, ffn_out, norm_params, cotangent
):
    row_count, local_len, model_width = tokens.shape
    total_len = local_len * lax.axis_size("seq")
    offset = lax.axis_index("seq") * local_len
    table = jnp.asarray(offset_table(total_len, SPAN, MAX_REL))
    doc_ends = jnp.cumsum(lengths, axis=1)
    positions = jnp.arange(total_len, dtype=jnp.int32)
    doc_ids = jnp.sum((positions[None, :, None] >= doc_ends[:, None, :]).astype(jnp.int32), axis=2)
    local_ids = lax.dynamic_slice_in_dim(doc_ids, offset, local_len, 1)
    same_doc = (local_ids[:, :, None] == doc_ids[:, None, :])[:, None]
    context = (same_doc, offset)
    stream = tokens.astype(jnp.float32)
    saved_layers = []
    for layer_num in range(2):
        norm_rows = norm_params[layer_num]
        middle_state, kept_attn = attention_forward(
            stream,
            qkv_weight[layer_num],
            out_weight[layer_num],
            rel_table[layer_num],
            norm_rows,
            context,
            table,
        )
        ffn_branch, kept_ffn = ffn_forward(middle_state, ffn_in[layer_num], ffn_out[layer_num])
        pre_norm = middle_state + ffn_branch
        saved_layers.append((kept_attn, kept_ffn, pre_norm))
        stream = layer_norm(pre_norm, norm_rows[2], norm_rows[3])
    d_stream = cotangent.astype(jnp.float32)
    grads_attn = []
    grads_ffn = []
    for layer_num in (1, 0):
        kept_attn, kept_ffn, pre_norm = saved_layers[layer_num]
        norm_rows = norm_params[layer_num]
        d_pre, d_gain_two, d_bias_two = norm_back(pre_norm, norm_rows[2], norm_rows[3], d_stream)
        d_middle, grad_in, grad_down = ffn_backward(d_pre.astype(jnp.bfloat16), kept_ffn)
        d_resid, d_gain_one, d_bias_one = norm_back(
            kept_attn[7], norm_rows[0], norm_rows[1], d_pre + d_middle
        )
        d_stream, grad_qkv, grad_out, grad_rel = attention_backward(
            d_resid,
            kept_attn,
            qkv_weight[layer_num],
            out_weight[layer_num],
            rel_table[layer_num],
            context,
            table,
        )
        grads_attn.insert(
            0,
            (
                grad_qkv,
                grad_out,
                grad_rel,
                jnp.stack([d_gain_one, d_bias_one, d_gain_two, d_bias_two]),
            ),
        )
        grads_ffn.insert(0, (grad_in, grad_down))
    all_qkv = jnp.stack([item[0] for item in grads_attn])
    all_out = jnp.stack([item[1] for item in grads_attn])
    all_rel = jnp.stack([item[2] for item in grads_attn])
    all_norm = jnp.stack([item[3] for item in grads_attn])
    all_in = jnp.stack([item[0] for item in grads_ffn])
    all_down = jnp.stack([item[1] for item in grads_ffn])
    all_qkv, all_out, all_rel, all_norm = (
        lax.psum_scatter(
            all_qkv.astype(jnp.bfloat16), "col", scatter_dimension=3, tiled=True
        ).astype(jnp.float32),
        lax.psum_scatter(
            all_out.astype(jnp.bfloat16), "col", scatter_dimension=2, tiled=True
        ).astype(jnp.float32),
        lax.psum_scatter(
            all_rel.astype(jnp.bfloat16), "col", scatter_dimension=2, tiled=True
        ).astype(jnp.float32),
        lax.psum_scatter(
            all_norm.astype(jnp.bfloat16), "col", scatter_dimension=1, tiled=True
        ).astype(jnp.float32),
    )
    all_qkv, all_out, all_rel, all_norm, all_in, all_down = (
        lax.psum_scatter(all_qkv, ("seq", "rows"), scatter_dimension=2, tiled=True),
        lax.psum_scatter(all_out, ("seq", "rows"), scatter_dimension=1, tiled=True),
        lax.psum_scatter(all_rel, ("seq", "rows"), scatter_dimension=1, tiled=True),
        lax.psum_scatter(all_norm, ("seq", "rows"), scatter_dimension=2, tiled=True),
        lax.psum_scatter(all_in, ("seq", "rows"), scatter_dimension=1, tiled=True),
        lax.psum_scatter(all_down, ("seq", "rows"), scatter_dimension=1, tiled=True),
    )
    return (stream, d_stream, all_qkv, all_out, all_rel, all_in, all_down, all_norm)


def solution(mesh):
    placed = (
        P(("rows", "col"), "seq", None),
        P(("rows", "col"), None),
        P(),
        P(),
        P(),
        P(None, None, "col"),
        P(None, None, "col"),
        P(),
        P(("rows", "col"), "seq", None),
    )
    return jax.shard_map(
        per_device,
        mesh=mesh,
        in_specs=placed,
        out_specs=(
            P(("rows", "col"), "seq", None),
            P(("rows", "col"), "seq", None),
            P(None, None, ("seq", "rows"), "col"),
            P(None, ("seq", "rows"), "col"),
            P(None, ("seq", "rows"), "col"),
            P(None, ("seq", "rows"), "col"),
            P(None, ("seq", "rows"), "col"),
            P(None, "col", ("seq", "rows")),
        ),
        check_vma=False,
    )
```

profile of v0, /device:TPU:0, one launch (start us, length us, event | category | flops | bytes accessed | tf_op | source)
XLA Modules:
  0.0 2248.2 jit_solution(14408326044254566438)
XLA Ops:
  11.3 12.7 all-gather
  24.0 6.9 convert_bitcast_fusion.1
  33.2 11.3 all-gather.1
  44.5 10.1 convolution_bitcast_fusion.1
  54.6 24.8 %copy.222 = f32[1,12,512,1024]{3,2,0,1:T(8,128)} copy(f32[1,12,512,1024]{2,3,1,0:T(8,128)} %convolution_bitcast_fusion.1) | data formatting | bytes 50331648 | tf_op jit(solution)/shard_map/rjhe,mhe->rhjm/transpose | solution.py:78
  79.4 33.2 %reshape.889 = f32[1,12,524288]{2,0,1:T(1,128)} reshape(f32[1,12,512,1024]{3,2,0,1:T(8,128)} %copy.222) | data formatting | bytes 50331648 | tf_op jit(solution)/shard_map/reshape | solution.py:63
  112.6 77.2 %fusion = f32[12,523776]{1,0:T(8,128)} fusion(s32[]{:T(128)S(6)} %select_n.52, f32[1,12,524288]{2,0,1:T(1,128)} %reshape.889), kind=kLoop, calls=%fused_computation.4 | loop fusion | bytes 50307076 | tf_op jit(solution)/shard_map/dynamic_slice | solution.py:65
  189.8 54.0 %reshape.890 = f32[1,12,512,1023]{3,2,0,1:T(8,128)} reshape(f32[12,523776]{1,0:T(8,128)} %fusion) | data formatting | bytes 50282496 | tf_op jit(solution)/shard_map/reshape | solution.py:66
  262.5 12.6 copy.220
  275.1 19.3 reshape.887
  294.4 39.5 %fusion.2 = f32[12,261888]{1,0:T(8,128)} fusion(s32[]{:T(128)S(6)} %select_n.51, f32[1,12,262144]{2,0,1:T(1,128)} %reshape.887), kind=kLoop, calls=%fused_computation.10 | loop fusion | bytes 25153540 | tf_op jit(solution)/shard_map/dynamic_slice | solution.py:65
  333.9 22.3 reshape.888
  369.8 21.0 all-gather.13.cloned.1.call-done
  390.7 10.9 fusion.44
  415.9 17.9 reduce-scatter.21.cloned.1.call-done
  440.0 11.5 all-gather.3
  452.7 10.8 all-gather.4
  464.9 10.5 convolution_bitcast_fusion
  475.5 24.8 %copy.230 = f32[1,12,512,1024]{3,2,0,1:T(8,128)} copy(f32[1,12,512,1024]{2,3,1,0:T(8,128)} %convolution_bitcast_fusion) | data formatting | bytes 50331648 | tf_op jit(solution)/shard_map/rjhe,mhe->rhjm/transpose | solution.py:78
  500.3 33.2 %reshape.901 = f32[1,12,524288]{2,0,1:T(1,128)} reshape(f32[1,12,512,1024]{3,2,0,1:T(8,128)} %copy.230) | data formatting | bytes 50331648 | tf_op jit(solution)/shard_map/reshape | solution.py:63
  533.5 77.2 %fusion.1 = f32[12,523776]{1,0:T(8,128)} fusion(s32[]{:T(128)S(6)} %select_n.52, f32[1,12,524288]{2,0,1:T(1,128)} %reshape.901), kind=kLoop, calls=%fused_computation.5 | loop fusion | bytes 50307076 | tf_op jit(solution)/shard_map/dynamic_slice | solution.py:65
  610.7 41.7 %reshape.902 = f32[1,12,512,1023]{3,2,0,1:T(8,128)} reshape(f32[12,523776]{1,0:T(8,128)} %fusion.1) | data formatting | bytes 50282496 | tf_op jit(solution)/shard_map/reshape | solution.py:66
  672.4 12.6 copy.228
  684.9 19.3 reshape.899
  704.3 39.5 %fusion.3 = f32[12,261888]{1,0:T(8,128)} fusion(s32[]{:T(128)S(6)} %select_n.51, f32[1,12,262144]{2,0,1:T(1,128)} %reshape.899), kind=kLoop, calls=%fused_computation.11 | loop fusion | bytes 25153540 | tf_op jit(solution)/shard_map/dynamic_slice | solution.py:65
  743.7 22.3 reshape.900
  779.3 19.8 all-gather.15.cloned.1.call-done
  799.0 10.9 fusion.47
  813.9 28.3 %reduce-scatter.23.cloned.1.call-done = bf16[256,768]{1,0:T(8,128)(2,1)} async-done(((bf16[1024,768]{1,0:T(8,128)(2,1)}), bf16[256,768]{1,0:T(8,128)(2,1)}) %reduce-scatter.23.cloned.1.call-update) | async-done | bytes 393232 | tf_op jit(solution)/shard_map/reduce_scatter | solution.py:243
  846.9 19.8 all-gather.17.cloned.1.call-done
  875.3 28.3 %reduce-scatter.25.cloned.1.call-done = bf16[256,768]{1,0:T(8,128)(2,1)} async-done(((bf16[1024,768]{1,0:T(8,128)(2,1)}), bf16[256,768]{1,0:T(8,128)(2,1)}) %reduce-scatter.25.cloned.1.call-update) | async-done | bytes 393232 | tf_op jit(solution)/shard_map/reduce_scatter | solution.py:267
  928.3 8.0 pad.54.clone
  936.4 34.8 %reshape.959 = bf16[1,12,523776]{2,1,0:T(8,128)(2,1)} reshape(bf16[1,12,512,1023]{3,2,0,1:T(8,128)(2,1)} %pad.54.clone) | data formatting | bytes 25141248 | tf_op jit(solution)/shard_map/transpose(jvp())/reshape | solution.py:66
  977.1 86.0 %dynamic_update_slice.13 = bf16[1,12,525312]{2,1,0:T(8,128)(2,1)} dynamic-update-slice(bf16[1,12,525312]{2,1,0:T(8,128)(2,1)} %broadcast.437.clone, bf16[1,12,523776]{2,1,0:T(8,128)(2,1)} %reshape.959, s32[]{:T(128)} %constant.46.clone.1, s32[]{:T(128)} %constant.46.clone.1, s32[]{:T(128)S(6)} %select_n.52) | dynamic-update-slice | bytes 25141252 | tf_op jit(solution)/shard_map/transpose(jvp())/dynamic_update_slice | solution.py:65
  1063.0 8.0 pad.201
  1071.0 21.1 copy.344
  1106.4 17.4 reshape.958
  1127.4 43.6 %dynamic_update_slice.12 = bf16[1,12,263168]{2,1,0:T(8,128)(2,1)} dynamic-update-slice(bf16[1,12,263168]{2,1,0:T(8,128)(2,1)} %broadcast.435.clone, bf16[1,12,261888]{2,1,0:T(8,128)(2,1)} %reshape.958, s32[]{:T(128)} %constant.46.clone.1, s32[]{:T(128)} %constant.46.clone.1, s32[]{:T(128)S(6)} %select_n.51) | dynamic-update-slice | bytes 12570628 | tf_op jit(solution)/shard_map/transpose(jvp())/dynamic_update_slice | solution.py:65
  1171.0 7.2 pad.203
  1178.2 11.4 copy.343
  1207.6 8.9 fusion.8
  1233.6 7.1 multiply_bitcast_fusion
  1283.0 8.0 pad.58.clone
  1291.0 34.8 %reshape.961 = bf16[1,12,523776]{2,1,0:T(8,128)(2,1)} reshape(bf16[1,12,512,1023]{3,2,0,1:T(8,128)(2,1)} %pad.58.clone) | data formatting | bytes 25141248 | tf_op jit(solution)/shard_map/transpose(jvp())/reshape | solution.py:66
  1331.7 86.0 %dynamic_update_slice.15 = bf16[1,12,525312]{2,1,0:T(8,128)(2,1)} dynamic-update-slice(bf16[1,12,525312]{2,1,0:T(8,128)(2,1)} %broadcast.437, bf16[1,12,523776]{2,1,0:T(8,128)(2,1)} %reshape.961, s32[]{:T(128)} %constant.46.clone.1, s32[]{:T(128)} %constant.46.clone.1, s32[]{:T(128)S(6)} %select_n.52) | dynamic-update-slice | bytes 25141252 | tf_op jit(solution)/shard_map/transpose(jvp())/dynamic_update_slice | solution.py:65
  1417.7 8.0 pad.200
  1425.7 21.1 copy.346
  1446.8 6.9 fusion.6
  1461.0 17.4 reshape.960
  1482.1 43.6 %dynamic_update_slice.14 = bf16[1,12,263168]{2,1,0:T(8,128)(2,1)} dynamic-update-slice(bf16[1,12,263168]{2,1,0:T(8,128)(2,1)} %broadcast.435, bf16[1,12,261888]{2,1,0:T(8,128)(2,1)} %reshape.960, s32[]{:T(128)} %constant.46.clone.1, s32[]{:T(128)} %constant.46.clone.1, s32[]{:T(128)S(6)} %select_n.51) | dynamic-update-slice | bytes 12570628 | tf_op jit(solution)/shard_map/transpose(jvp())/dynamic_update_slice | solution.py:65
  1525.6 7.2 pad.202
  1532.9 11.4 copy.345
  1619.7 11.9 all-reduce.11
  1634.5 47.1 %all-reduce.18.cloned.1.call-done = (bf16[2,768,768]{1,0,2:T(2,128)(2,1)}, bf16[2,512,768]{1,0,2:T(2,128)(2,1)}) async-done(((bf16[2,768,768]{1,0,2:T(2,128)(2,1)}, bf16[2,512,768]{1,0,2:T(2,128)(2,1)}), (bf16[2,768,768]{1,0,2:T(2,128)(2,1)}, bf16[2,512,768]{1,0,2:T(2,128)(2,1)})) %all-reduce.18.cloned.1.call-update) | async-done | bytes 3932176
  1685.8 36.8 %copy.278 = f32[2,768,192]{0,2,1:T(8,128)} copy(f32[2,768,192]{1,0,2:T(2,128)S(1)} %dynamic-slice_convert_fusion) | data formatting | bytes 2359296
  1722.6 52.0 %reshape.964 = f32[768,384]{1,0:T(8,128)} reshape(f32[768,192,2]{2,1,0:T(8,128)} %bitcast.158) | data formatting | bytes 2359296
  1781.1 8.0 reshape.962
  1818.7 75.4 %all-reduce.16.cloned.1.call-done = f32[2,512,192]{2,0,1:T(2,128)} async-done(((f32[2,512,192]{2,0,1:T(2,128)}), f32[2,512,192]{2,0,1:T(2,128)}) %all-reduce.16.cloned.1.call-update) | async-done | bytes 786448
  1895.7 65.4 %reduce-scatter.45.cloned.1.call-done = f32[96,384]{1,0:T(8,128)} async-done(((f32[768,384]{1,0:T(8,128)}), f32[96,384]{1,0:T(8,128)}) %reduce-scatter.45.cloned.1.call-update) | async-done | bytes 147472
  1961.1 11.7 reshape.965
  1972.8 6.9 copy.263
  1979.7 63.0 %reduce-scatter.43.cloned.1.call-done = f32[96,1152]{1,0:T(8,128)} async-done(((f32[768,1152]{1,0:T(8,128)}), f32[96,1152]{1,0:T(8,128)}) %reduce-scatter.43.cloned.1.call-update) | async-done | bytes 442384
  2045.3 96.7 %reduce-scatter.39.cloned.1.call-done = f32[2,96,768]{2,1,0:T(8,128)} async-done(((f32[2,768,768]{2,1,0:T(8,128)}), f32[2,96,768]{2,1,0:T(8,128)}) %reduce-scatter.39.cloned.1.call-update) | async-done | bytes 589840 | tf_op jit(solution)/shard_map/reduce_scatter | solution.py:363
  2141.9 99.2 %reduce-scatter.41.cloned.1.call-done = f32[2,96,768]{2,1,0:T(8,128)} async-done(((f32[2,768,768]{2,1,0:T(8,128)}), f32[2,96,768]{2,1,0:T(8,128)}) %reduce-scatter.41.cloned.1.call-update) | async-done | bytes 589840 | tf_op jit(solution)/shard_map/reduce_scatter | solution.py:364
  (468 shorter events, 374.5 us)
Async XLA Ops:
  7.2 383.6 %all-gather.13.cloned.1.call-start = ((), (), s32[]{:S(2)}) async-start(), calls=%async_computation.25 | async-start | bytes 1966080 | tf_op jit(solution)/shard_map/all_gather | solution.py:240
  10.4 13.6 copy-start.32
  11.3 345.5 %copy-start.19 = (bf16[1,1,256,768]{2,3,0,1:T(8,128)(2,1)}, bf16[1,1,256,768]{2,3,0,1:T(8,128)(2,1)S(1)}, u32[]{:S(2)}) copy-start(bf16[1,1,256,768]{2,3,0,1:T(8,128)(2,1)S(1)} %get-tuple-element.97) | copy-start | bytes 1179652
  24.0 342.0 %copy-start.25 = (bf16[1,1,512,768]{2,3,0,1:T(8,128)(2,1)}, bf16[1,1,512,768]{2,3,0,1:T(8,128)(2,1)S(1)}, u32[]{:S(2)}) copy-start(bf16[1,1,512,768]{2,3,0,1:T(8,128)(2,1)S(1)} %all-gather) | copy-start | bytes 2359300
  33.2 11.4 copy-start.15
  33.2 223.0 %copy-start.28 = (bf16[1,1024,768]{1,2,0:T(8,128)(2,1)}, bf16[1,1024,768]{1,2,0:T(8,128)(2,1)S(1)}, u32[]{:S(2)}) copy-start(bf16[1,1024,768]{1,2,0:T(8,128)(2,1)S(1)} %get-tuple-element.92) | copy-start | bytes 4718596
  44.5 312.2 %copy-start.4 = (bf16[1,1,512,768]{2,3,0,1:T(8,128)(2,1)}, bf16[1,1,512,768]{2,3,0,1:T(8,128)(2,1)S(1)}, u32[]{:S(2)}) copy-start(bf16[1,1,512,768]{2,3,0,1:T(8,128)(2,1)S(1)} %all-gather.1) | copy-start | bytes 2359300
  333.9 22.3 copy-start.115
  356.7 6.6 copy-start.50
  366.0 67.8 %copy-start.60 = (f32[768]{0:T(1024)}, f32[768]{0:T(1024)S(1)}, u32[]{:S(2)}) copy-start(f32[768]{0:T(1024)S(1)} %get-tuple-element.73) | copy-start | bytes 9220
  366.0 69.5 %copy-start.74 = (f32[768]{0:T(1024)}, f32[768]{0:T(1024)S(1)}, u32[]{:S(2)}) copy-start(f32[768]{0:T(1024)S(1)} %get-tuple-element.71) | copy-start | bytes 9220
  366.0 69.5 %copy-start.96 = (f32[768]{0:T(1024)}, f32[768]{0:T(1024)S(1)}, u32[]{:S(2)}) copy-start(f32[768]{0:T(1024)S(1)} %get-tuple-element.70) | copy-start | bytes 9220
  367.9 33.8 %copy-start.45 = (bf16[12,64,256]{2,1,0:T(8,128)(2,1)}, bf16[12,64,256]{2,1,0:T(8,128)(2,1)S(1)}, u32[]{:S(2)}) copy-start(bf16[12,64,256]{2,1,0:T(8,128)(2,1)S(1)} %convolution_convert_fusion.11) | copy-start | bytes 1179652
  368.5 65.4 %copy-start.10 = (f32[1,256,768]{2,1,0:T(8,128)}, f32[1,256,768]{2,1,0:T(8,128)S(1)}, u32[]{:S(2)}) copy-start(f32[1,256,768]{2,1,0:T(8,128)S(1)} %get-tuple-element.103) | copy-start | bytes 2359300
  368.5 65.3 %copy-start.64 = (f32[256]{0:T(256)}, f32[256]{0:T(256)S(1)}, u32[]{:S(2)}) copy-start(f32[256]{0:T(256)S(1)} %broadcast_multiply_fusion.3) | copy-start | bytes 3076
  368.7 32.9 %copy-start.81 = (f32[256]{0:T(256)}, f32[256]{0:T(256)S(1)}, u32[]{:S(2)}) copy-start(f32[256]{0:T(256)S(1)} %multiply_reduce_fusion.9) | copy-start | bytes 3076
  368.8 65.1 %copy-start.69 = (f32[256]{0:T(256)}, f32[256]{0:T(256)S(1)}, u32[]{:S(2)}) copy-start(f32[256]{0:T(256)S(1)} %fusion.280) | copy-start | bytes 3076
  369.7 64.1 %reduce-scatter.21.cloned.1.call-start = ((), (), s32[]{:S(2)}) async-start(), calls=%async_computation.14 | async-start | bytes 1966080 | tf_op jit(solution)/shard_map/reduce_scatter | solution.py:243
  390.7 12.1 copy-start.101
  405.5 393.5 %all-gather.15.cloned.1.call-start = ((), (), s32[]{:S(2)}) async-start(), calls=%async_computation.26 | async-start | bytes 1966080 | tf_op jit(solution)/shard_map/all_gather | solution.py:240
  415.9 49.0 %copy-start.17 = (bf16[1,1024,768]{1,2,0:T(8,128)(2,1)}, bf16[1,1024,768]{1,2,0:T(8,128)(2,1)S(1)}, u32[]{:S(2)}) copy-start(bf16[1,1024,768]{1,2,0:T(8,128)(2,1)S(1)} %get-tuple-element.89) | copy-start | bytes 4718596
  435.2 342.1 %copy-start.22 = (f32[1,256,768]{2,1,0:T(8,128)}, f32[1,256,768]{2,1,0:T(8,128)S(1)}, u32[]{:S(2)}) copy-start(f32[1,256,768]{2,1,0:T(8,128)S(1)} %get-tuple-element.88) | copy-start | bytes 2359300
  464.9 301.1 %copy-start.6 = (bf16[1,1,512,768]{2,3,1,0:T(8,128)(2,1)}, bf16[1,1,512,768]{2,3,1,0:T(8,128)(2,1)S(1)}, u32[]{:S(2)}) copy-start(bf16[1,1,512,768]{2,3,1,0:T(8,128)(2,1)S(1)} %copy.226) | copy-start | bytes 2359300
  658.2 7.8 copy-start.30
  743.7 22.3 copy-start.51
  777.3 32.7 %copy-start.47 = (bf16[12,64,256]{2,1,0:T(8,128)(2,1)}, bf16[12,64,256]{2,1,0:T(8,128)(2,1)S(1)}, u32[]{:S(2)}) copy-start(bf16[12,64,256]{2,1,0:T(8,128)(2,1)S(1)} %convolution_convert_fusion.10) | copy-start | bytes 1179652
  778.0 125.7 %copy-start.66 = (f32[256]{0:T(256)}, f32[256]{0:T(256)S(1)}, u32[]{:S(2)}) copy-start(f32[256]{0:T(256)S(1)} %broadcast_multiply_fusion.1) | copy-start | bytes 3076
  778.2 125.4 %copy-start.71 = (f32[256]{0:T(256)}, f32[256]{0:T(256)S(1)}, u32[]{:S(2)}) copy-start(f32[256]{0:T(256)S(1)} %fusion.282) | copy-start | bytes 3076
  779.2 62.9 %reduce-scatter.23.cloned.1.call-start = ((), (), s32[]{:S(2)}) async-start(), calls=%async_computation.15 | async-start | bytes 1966080 | tf_op jit(solution)/shard_map/reduce_scatter | solution.py:243
  799.0 12.1 copy-start.102
  813.8 29.9 %copy-start.39 = (bf16[1,256,768]{2,1,0:T(8,128)(2,1)S(1)}, bf16[1,256,768]{2,1,0:T(8,128)(2,1)}, u32[]{:S(2)}) copy-start(bf16[1,256,768]{2,1,0:T(8,128)(2,1)} %param.18) | copy-start | bytes 1179652
  813.8 29.9 %copy-start.67 = (f32[768]{0:T(1024)S(1)}, f32[768]{0:T(1024)}, u32[]{:S(2)}) copy-start(f32[768]{0:T(1024)} %get-tuple-element.67) | copy-start | bytes 9220
  813.8 30.9 %copy-start.77 = (f32[768]{0:T(1024)S(1)}, f32[768]{0:T(1024)}, u32[]{:S(2)}) copy-start(f32[768]{0:T(1024)} %get-tuple-element.74) | copy-start | bytes 9220
  813.8 52.8 %all-gather.17.cloned.1.call-start = ((), (), s32[]{:S(2)}) async-start(), calls=%async_computation.27 | async-start | bytes 1966080 | tf_op jit(solution)/shard_map/all_gather | solution.py:259
  846.0 57.7 %copy-start.73 = (f32[256]{0:T(256)}, f32[256]{0:T(256)S(1)}, u32[]{:S(2)}) copy-start(f32[256]{0:T(256)S(1)} %negate_multiply_fusion.5) | copy-start | bytes 3076
  846.8 56.8 %reduce-scatter.25.cloned.1.call-start = ((), (), s32[]{:S(2)}) async-start(), calls=%async_computation.16 | async-start | bytes 1966080 | tf_op jit(solution)/shard_map/reduce_scatter | solution.py:267
  872.6 31.0 %copy-start.63 = (f32[768]{0:T(1024)S(1)}, f32[768]{0:T(1024)}, u32[]{:S(2)}) copy-start(f32[768]{0:T(1024)} %get-tuple-element.69) | copy-start | bytes 9220
  875.3 321.0 %reduce-scatter.29.cloned.1.call-start = ((), (), s32[]{:S(2)}) async-start(), calls=%async_computation.18 | async-start | bytes 1179648 | tf_op jit(solution)/shard_map/reduce_scatter | solution.py:216
  920.0 276.3 %reduce-scatter.27.cloned.1.call-start = ((), (), s32[]{:S(2)}) async-start(), calls=%async_computation.17 | async-start | bytes 1179648 | tf_op jit(solution)/shard_map/reduce_scatter | solution.py:210
  1071.0 21.1 copy-start.18
  1102.9 118.7 %all-gather.19.cloned.1.call-start = ((), (), s32[]{:S(2)}) async-start(), calls=%async_computation.28 | async-start | bytes 1966080 | tf_op jit(solution)/shard_map/all_gather | solution.py:259
  1178.2 11.5 copy-start.7
  1201.8 56.8 %reduce-scatter.31.cloned.1.call-start = ((), (), s32[]{:S(2)}) async-start(), calls=%async_computation.19 | async-start | bytes 1966080 | tf_op jit(solution)/shard_map/reduce_scatter | solution.py:267
  1230.3 377.3 %reduce-scatter.35.cloned.1.call-start = ((), (), s32[]{:S(2)}) async-start(), calls=%async_computation.21 | async-start | bytes 1179648 | tf_op jit(solution)/shard_map/reduce_scatter | solution.py:216
  1233.6 7.1 copy-start.9
  1240.8 6.5 slice-start
  1261.7 10.2 copy-start.41
  1261.7 10.2 copy-start.88
  1274.7 333.0 %reduce-scatter.33.cloned.1.call-start = ((), (), s32[]{:S(2)}) async-start(), calls=%async_computation.20 | async-start | bytes 1179648 | tf_op jit(solution)/shard_map/reduce_scatter | solution.py:210
  1425.7 21.1 copy-start.16
  1446.8 6.9 copy-start.20
  1548.4 6.3 copy-start.5
  1567.0 114.6 %all-reduce.18.cloned.1.call-start = ((), (), s32[]{:S(2)}) async-start(), calls=%async_computation.33 | async-start | bytes 7864320
  1599.7 175.0 %reduce-scatter.37.cloned.1.call-start = ((), (), s32[]{:S(2)}) async-start(), calls=%async_computation.22 | async-start | bytes 8847360 | tf_op jit(solution)/shard_map/reduce_scatter | solution.py:345
  1617.2 195.9 %reduce-scatter.47.cloned.1.call-start = ((), (), s32[]{:S(2)}) async-start(), calls=%async_computation.31 | async-start | bytes 442368
  1634.5 259.6 %all-reduce.16.cloned.1.call-start = ((), (), s32[]{:S(2)}) async-start(), calls=%async_computation.32 | async-start | bytes 2097152
  1684.3 276.8 %reduce-scatter.45.cloned.1.call-start = ((), (), s32[]{:S(2)}) async-start(), calls=%async_computation.30 | async-start | bytes 1327104
  1774.7 268.0 %reduce-scatter.43.cloned.1.call-start = ((), (), s32[]{:S(2)}) async-start(), calls=%async_computation.29 | async-start | bytes 3981312
  1789.1 352.8 %reduce-scatter.39.cloned.1.call-start = ((), (), s32[]{:S(2)}) async-start(), calls=%async_computation.23 | async-start | bytes 5308416 | tf_op jit(solution)/shard_map/reduce_scatter | solution.py:363
  1797.5 443.7 %reduce-scatter.41.cloned.1.call-start = ((), (), s32[]{:S(2)}) async-start(), calls=%async_computation.24 | async-start | bytes 5308416 | tf_op jit(solution)/shard_map/reduce_scatter | solution.py:364
  1805.8 8.9 copy-start.42
  1805.8 8.9 copy-start.56
  1805.8 8.9 copy-start.57
  1805.8 8.9 copy-start.89
  (82 other events, 239.4 us)
Sparse Core Ops, SparseCore 0:
  369.9 20.8 all-gather.12
  405.6 28.1 reduce-scatter.20
  779.3 19.6 all-gather.14
  813.9 28.1 reduce-scatter.22
  847.0 19.6 all-gather.16
  875.4 28.1 reduce-scatter.24
  920.1 17.4 reduce-scatter.28
  1103.0 17.4 reduce-scatter.26
  1201.9 19.6 all-gather.18
  1230.4 28.1 reduce-scatter.30
  1274.8 17.4 reduce-scatter.34
  1567.1 17.4 reduce-scatter.32
  1599.9 81.6 all-reduce.17
  1684.0 63.7 reduce-scatter.36
  1751.8 61.2 reduce-scatter.46
  1816.8 77.1 all-reduce.15
  1897.3 63.7 reduce-scatter.44
  1964.6 78.0 reduce-scatter.42
  2046.9 94.9 reduce-scatter.38
  2146.0 95.1 reduce-scatter.40
where the time goes:
time: 2260 us; the launch traced here: 2250 us
  local copies, waits for them, and re-layouts  1270 us (56%)
  waiting for transfers between devices  594 us (26%)
  matrix products  264 us (12%)
  blocking collectives  58.3 us (3%)
  other arithmetic  45.4 us (2%)
    dynamic_update_slice x4, local copies, waits for them, and re-layouts, skew_rows(): part = lax.dynamic_slice_in_dim(flat, shift, count * (width - 1), len(lead))  259 us
    unnamed x25, waiting for transfers between devices  257 us
    reshape x8, local copies, waits for them, and re-layouts, skew_rows(): return part.reshape(lead + (count, width - 1))[..., :length]  245 us
    dynamic_slice x4, local copies, waits for them, and re-layouts, skew_rows(): part = lax.dynamic_slice_in_dim(flat, shift, count * (width - 1), len(lead))  233 us
    unnamed x277, local copies, waits for them, and re-layouts  231 us
    reshape x4, local copies, waits for them, and re-layouts, skew_rows(): flat = source.reshape(lead + (count * width,))  105 us
    reduce_scatter x1, waiting for transfers between devices, per_device(): lax.psum_scatter(all_down, ('seq', 'rows'), scatter_dimension=1, tiled=True)  99.2 us
    reduce_scatter x1, waiting for transfers between devices, per_device(): lax.psum_scatter(all_in, ('seq', 'rows'), scatter_dimension=1, tiled=True)  96.7 us
  transfers between devices with their start and end apart: 20, of which 15 were waited for; matrix products, arithmetic and copies ran while one was open for 36% of the time, Pallas kernels for 0%

commit v1 on v0

v1 whole, which is shorter than its diff:
```python
import functools
import jax
import jax.numpy as jnp
import numpy as np
from jax import lax
from jax.experimental import pallas as pl
from jax.experimental.pallas import tpu as pltpu
from jax.sharding import PartitionSpec as P

HEAD_DIM = 64
SPAN = 256
MAX_REL = 512
WIDE = 640
HALF = 320
BF = jnp.bfloat16
F32 = jnp.float32
SCALE = (3.0 * HEAD_DIM) ** (-0.5)
LOG2E = 1.4426950408889634

NT = (((1,), (1,)), ((), ()))
NN = (((1,), (0,)), ((), ()))
TN = (((0,), (0,)), ((), ()))

def dot(a, b, dims=NN):
    return lax.dot_general(a, b, dims, preferred_element_type=F32)

def bucket_table():
    r = HALF - np.arange(WIDE)
    middle = SPAN // 2
    a = np.where((r < middle) & (r > -middle), middle - 1, np.abs(r))
    logp = np.ceil(np.log(a / middle) / np.log((MAX_REL - 1) / middle) * (middle - 1)) + middle
    b = np.where(a <= middle, r, logp * np.sign(r))
    b = np.clip(b + SPAN, 0, 2 * SPAN - 1).astype(np.int32)
    return (b[:, None] == np.arange(2 * SPAN)[None, :]).astype(np.float32)

def fwd_kernel(ends_ref, x_ref, w_ref, pe_ref, rev_ref, o_ref, sv_ref, p_ref, bt_ref, sb_ref, *, length, blk):
    e1, e2, e3 = ends_ref[0], ends_ref[1], ends_ref[2]
    qkv = dot(x_ref[...], w_ref[0]).astype(BF)
    q, k, v = qkv[:, :128], qkv[:, 128:256], qkv[:, 256:]
    sv_ref[0, :, :128] = q
    sb_ref[...] = qkv
    sv_ref[0, :, 128:] = dot(rev_ref[...], qkv[:, 128:]).astype(BF)
    lane = lax.broadcasted_iota(jnp.int32, (1, 128), 1)
    posj = lax.broadcasted_iota(jnp.int32, (1, length), 1)
    idj = (posj >= e1).astype(jnp.int32) + (posj >= e2).astype(jnp.int32) + (posj >= e3).astype(jnp.int32)
    for h in range(2):
        own = (lane < 64) if h == 0 else (lane >= 64)
        kh = jnp.where(own, sb_ref[:, 128:256], jnp.zeros((), BF))
        for b in range(length // blk):
            sl = slice(b * blk, (b + 1) * blk)
            t2 = dot(kh[sl], pe_ref[0, 0], NT)
            t2 = pltpu.roll(t2, (b * blk + HALF) % WIDE, 1, stride=1, stride_axis=0)
            bt_ref[:, sl] = t2[:, :length].T
        for b in range(length // blk):
            sl = slice(b * blk, (b + 1) * blk)
            qb = jnp.where(own, sb_ref[sl, :128], jnp.zeros((), BF))
            t1 = dot(qb, pe_ref[0, 1], NT)
            t1 = pltpu.roll(t1, (b * blk + HALF) % WIDE, 1, stride=1, stride_axis=0)
            s = dot(qb, sb_ref[:, 128:256], NT) + t1[:, :length] + bt_ref[sl, :]
            posi = lax.broadcasted_iota(jnp.int32, (blk, 1), 0) + b * blk
            idi = (posi >= e1).astype(jnp.int32) + (posi >= e2).astype(jnp.int32) + (posi >= e3).astype(jnp.int32)
            s = jnp.where(idi == idj, s, -1e30)
            m = jnp.max(s, axis=1, keepdims=True)
            e = jnp.exp2((s - m) * (SCALE * LOG2E))
            p = (e * (1.0 / jnp.sum(e, axis=1, keepdims=True))).astype(BF)
            o = dot(p, sb_ref[:, 256:])
            if h == 0:
                o_ref[sl, :] = o.astype(BF)
            else:
                o_ref[sl, :] = jnp.where(own, o.astype(BF), o_ref[sl, :])
            p_ref[h, sl, :] = dot(p, rev_ref[...]).astype(BF)

def attn_fwd(ends, x, w, pe, rev):
    length = x.shape[0]
    model = x.shape[1]
    pairs = w.shape[0]
    return pl.pallas_call(
        functools.partial(fwd_kernel, length=length, blk=128),
        out_shape=(
            jax.ShapeDtypeStruct((length, pairs * 128), BF),
            jax.ShapeDtypeStruct((pairs, length, 384), BF),
            jax.ShapeDtypeStruct((2 * pairs, length, length), BF),
        ),
        grid_spec=pltpu.PrefetchScalarGridSpec(
            num_scalar_prefetch=1,
            grid=(pairs,),
            in_specs=[
                pl.BlockSpec((length, model), lambda g, e: (0, 0)),
                pl.BlockSpec((1, model, 384), lambda g, e: (g, 0, 0)),
                pl.BlockSpec((1, 2, WIDE, 128), lambda g, e: (g, 0, 0, 0)),
                pl.BlockSpec((length, length), lambda g, e: (0, 0)),
            ],
            out_specs=(
                pl.BlockSpec((length, 128), lambda g, e: (0, g)),
                pl.BlockSpec((1, length, 384), lambda g, e: (g, 0, 0)),
                pl.BlockSpec((2, length, length), lambda g, e: (g, 0, 0)),
            ),
            scratch_shapes=[pltpu.VMEM((length, length), F32), pltpu.VMEM((length, 384), BF)],
        ),
        compiler_params=pltpu.CompilerParams(vmem_limit_bytes=48 << 20),
        name="attention",
    )(ends, x, w, pe, rev)


def bwd_kernel(drb_ref, wo_ref, sv_ref, p_ref, pe_ref, rev_ref, wt_ref, dq_ref, dpe_ref, dx_ref, dt_ref, u_ref, acc_ref, *, length, blk):
    g = pl.program_id(0)
    lane = lax.broadcasted_iota(jnp.int32, (1, 128), 1)
    zero = jnp.zeros((), BF)
    dO = dot(drb_ref[...], wo_ref[...], NT).astype(BF)
    q = sv_ref[0, :, :128]
    dOT, qT, krT = dO.T, q.T, sv_ref[0, :, 128:256].T
    nb = length // blk
    for h in range(2):
        own = (lane < 64) if h == 0 else (lane >= 64)
        hs = slice(64 * h, 64 * h + 64)
        krh = jnp.where(own, sv_ref[0, :, 128:256], zero)
        pkh = jnp.where(own, pe_ref[0, 1], zero)
        for b in range(nb):
            sl = slice(b * blk, (b + 1) * blk)
            dOb = jnp.where(own, dO[sl], zero)
            da = dot(dOb, sv_ref[0, :, 256:], NT)
            p = p_ref[h, sl, :].astype(F32)
            delta = jnp.sum(p * da, axis=1, keepdims=True)
            ds = p * (da - delta)
            dsb = ds.astype(BF)
            ds = dsb.astype(F32)
            dt_ref[:, sl] = ds.T
            u = jnp.concatenate([ds, jnp.zeros((blk, WIDE - length), F32)], axis=1)
            u = pltpu.roll(u, (b * blk + WIDE - 192) % WIDE, 1, stride=1, stride_axis=0).astype(BF)
            u_ref[sl, :] = u
            r = dot(dsb, krh) + dot(u, pkh)
            if h == 0:
                acc_ref[sl, :128] = r
            else:
                acc_ref[sl, :128] = acc_ref[sl, :128] + r
        dpe_ref[0, 1, hs, :] = dot(qT[hs], u_ref[...])
        acc_ref[:, 256:384] = (acc_ref[:, 256:384] if h else 0.0) + dot(p_ref[h], jnp.where(own, dO, zero), TN)
        qh = jnp.where(own, q, zero)
        pqh = jnp.where(own, pe_ref[0, 0], zero)
        for b in range(nb):
            sl = slice(b * blk, (b + 1) * blk)
            z = dt_ref[sl, :]
            w = jnp.concatenate([z, jnp.zeros((blk, WIDE - length), F32)], axis=1)
            w = pltpu.roll(w, (b * blk + WIDE - 191) % WIDE, 1, stride=1, stride_axis=0).astype(BF)
            u_ref[sl, :] = w
            r = dot(z.astype(BF), qh) + dot(w, pqh)
            if h == 0:
                acc_ref[sl, 128:256] = r
            else:
                acc_ref[sl, 128:256] = acc_ref[sl, 128:256] + r
        dpe_ref[0, 0, hs, :] = dot(krT[hs], u_ref[...])
    dq = (acc_ref[:, :128] * SCALE).astype(BF)
    dk = (acc_ref[:, 128:256] * SCALE).astype(BF)
    dv = acc_ref[:, 256:384].astype(BF)
    dkv = dot(rev_ref[...], jnp.concatenate([dk, dv], axis=1)).astype(BF)
    dqkv = jnp.concatenate([dq, dkv], axis=1)
    dq_ref[0] = dqkv
    part = dot(dqkv, wt_ref[0], NT)
    @pl.when(g == 0)
    def _():
        dx_ref[...] = part
    @pl.when(g > 0)
    def _():
        dx_ref[...] = dx_ref[...] + part

def attn_bwd(drb, wo, saved, probs, pe, rev, w):
    length, model = drb.shape
    pairs = w.shape[0]
    return pl.pallas_call(
        functools.partial(bwd_kernel, length=length, blk=128),
        out_shape=(
            jax.ShapeDtypeStruct((pairs, length, 384), BF),
            jax.ShapeDtypeStruct((pairs, 2, 128, WIDE), F32),
            jax.ShapeDtypeStruct((length, model), F32),
        ),
        grid=(pairs,),
        in_specs=[
            pl.BlockSpec((length, model), lambda g: (0, 0)),
            pl.BlockSpec((128, model), lambda g: (g, 0)),
            pl.BlockSpec((1, length, 384), lambda g: (g, 0, 0)),
            pl.BlockSpec((2, length, length), lambda g: (g, 0, 0)),
            pl.BlockSpec((1, 2, WIDE, 128), lambda g: (g, 0, 0, 0)),
            pl.BlockSpec((length, length), lambda g: (0, 0)),
            pl.BlockSpec((1, model, 384), lambda g: (g, 0, 0)),
        ],
        out_specs=(
            pl.BlockSpec((1, length, 384), lambda g: (g, 0, 0)),
            pl.BlockSpec((1, 2, 128, WIDE), lambda g: (g, 0, 0, 0)),
            pl.BlockSpec((length, model), lambda g: (0, 0)),
        ),
        scratch_shapes=[pltpu.VMEM((length, length), F32), pltpu.VMEM((length, WIDE), BF), pltpu.VMEM((length, 384), F32)],
        compiler_params=pltpu.CompilerParams(vmem_limit_bytes=48 << 20),
        name="attention_grad",
    )(drb, wo, saved, probs, pe, rev, w)

EPSILON = 1e-07


def layer_norm(stream, gain_row, bias_row):
    row_mean = jnp.mean(stream, axis=-1, keepdims=True)
    centered = stream - row_mean
    row_var = jnp.mean(centered * centered, axis=-1, keepdims=True)
    return centered * lax.rsqrt(row_var + EPSILON) * gain_row + bias_row


def norm_back(state, gain_row, bias_row, d_result):
    unused_out, pull_back = jax.vjp(layer_norm, state, gain_row, bias_row)
    return pull_back(d_result)


def gelu_slope(hidden):
    cumulative = 0.5 * (1.0 + lax.erf(hidden * 0.7071067811865476))
    density = jnp.exp(-0.5 * hidden * hidden) * 0.3989422804014327
    return cumulative + hidden * density


class Wires:
    def __init__(self):
        self.seqs = lax.axis_size("seq")
        self.rows = lax.axis_size("rows")
        self.cols = lax.axis_size("col")
        self.seq = lax.axis_index("seq")
        self.row = lax.axis_index("rows")
        self.col = lax.axis_index("col")
        self.core = self.col % 2

    def send(self, array, target):
        pairs = []
        for s in range(self.seqs):
            for r in range(self.rows):
                for c in range(self.cols):
                    t = target(s, r, c)
                    if t is not None:
                        pairs.append(((s * self.rows + r) * self.cols + c, (t[0] * self.rows + t[1]) * self.cols + t[2]))
        return lax.ppermute(array, ("seq", "rows", "col"), pairs)

    def turn(self, array):
        return self.send(array, lambda s, r, c: (c % 2, r, c - c % 2 + s))

    def core_swap(self, array):
        return self.send(array, lambda s, r, c: (s, r, c ^ 1))

    def in_order(self, own, other, axis):
        first = self.core == 0
        return jnp.concatenate([jnp.where(first, own, other), jnp.where(first, other, own)], axis=axis)


def ffn_forward(middle_state, w_in, w_down):
    ffn_rows = middle_state.astype(BF)
    gathered = lax.all_gather(ffn_rows, "col", axis=0, tiled=True)
    hidden = jnp.dot(gathered, w_in, preferred_element_type=F32)
    activated = jax.nn.gelu(hidden, approximate=False).astype(BF)
    part = jnp.einsum("tf,df->td", activated, w_down, preferred_element_type=F32).astype(BF)
    branch = lax.psum_scatter(part, "col", scatter_dimension=0, tiled=True).astype(F32)
    return branch, gathered


def ffn_backward(d_rows, source_rows, w_in, w_down):
    cot_rows = lax.all_gather(d_rows, "col", axis=0, tiled=True)
    hidden = jnp.dot(source_rows, w_in, preferred_element_type=F32)
    activated = jax.nn.gelu(hidden, approximate=False).astype(BF)
    d_hidden = (jnp.dot(cot_rows, w_down, preferred_element_type=F32) * gelu_slope(hidden)).astype(BF)
    grad_down = jnp.einsum("td,tf->df", cot_rows, activated, preferred_element_type=F32)
    grad_in = jnp.einsum("td,tf->df", source_rows, d_hidden, preferred_element_type=F32)
    part = jnp.einsum("tf,df->td", d_hidden, w_in, preferred_element_type=F32).astype(BF)
    d_middle = lax.psum_scatter(part, "col", scatter_dimension=0, tiled=True).astype(F32)
    return d_middle, grad_in, grad_down


def per_device(tokens, lengths, qkv_weight, out_weight, rel_table, ffn_in, ffn_out, norm_params, cotangent):
    wires = Wires()
    core = wires.core
    local, model = tokens.shape[1:]
    length = 2 * local
    layers = qkv_weight.shape[0]
    half = model // 2
    block = model // wires.cols
    pairs = half // 128
    table = jnp.asarray(bucket_table(), BF)
    rev = jnp.asarray(np.eye(length)[::-1], BF)
    start = wires.turn(tokens[0])
    ends = jnp.cumsum(wires.turn(lengths)[0])
    d_final = wires.turn(cotangent[0])

    def own_blocks(array, axis, which):
        shape = array.shape
        cut = array.reshape(shape[:axis] + (wires.cols // 2, 2, block) + shape[axis + 1:])
        cut = lax.dynamic_index_in_dim(cut, which, axis + 1, keepdims=False)
        return cut.reshape(shape[:axis] + (half,) + shape[axis + 1:])

    qkv_own = own_blocks(qkv_weight, 3, core)
    out_own = own_blocks(out_weight, 1, core)
    out_other = own_blocks(out_weight, 1, 1 - core)
    w_pairs = qkv_own.reshape(layers, 3, model, pairs, 128).transpose(0, 3, 2, 1, 4).reshape(layers, pairs, model, 384)
    pos = jnp.einsum("nbd,ncde->ncbe", rel_table, qkv_own[:, :2], preferred_element_type=F32).astype(BF)
    ext = jnp.einsum("ub,ncbe->ncue", table, pos, preferred_element_type=F32).astype(BF)
    pe_fwd = ext.reshape(layers, 2, WIDE, pairs, 128).transpose(0, 3, 1, 2, 4)
    ext_b = jnp.einsum("ub,nbe->nue", table[::-1], pos[:, 1], preferred_element_type=F32).astype(BF)
    pe_bwd = jnp.stack([ext[:, 0], ext_b], axis=1).reshape(layers, 2, WIDE, pairs, 128).transpose(0, 3, 1, 2, 4)

    stream = start.astype(F32)
    kept = []
    for n in range(layers):
        norm_rows = norm_params[n]
        x_own = stream.astype(BF)
        x_full = wires.in_order(x_own, wires.core_swap(x_own), 0)
        o_own, saved, probs = attn_fwd(ends, x_full, w_pairs[n], pe_fwd[n], rev)
        o_other = wires.core_swap(o_own)
        o_mine = lax.dynamic_slice_in_dim(o_own, core * local, local, 0)
        o_rest = lax.dynamic_slice_in_dim(o_other, core * local, local, 0)
        branch = dot(o_mine, out_own[n]) + dot(o_rest, out_other[n])
        resid = stream + branch
        middle = layer_norm(resid, norm_rows[0], norm_rows[1])
        ffn_branch, gathered = ffn_forward(middle, ffn_in[n], ffn_out[n])
        pre_norm = middle + ffn_branch
        stream = layer_norm(pre_norm, norm_rows[2], norm_rows[3])
        kept.append((x_full, o_own, o_other, saved, probs, resid, gathered, pre_norm))
    output = wires.turn(stream)
    d_stream = d_final.astype(F32)
    grads = [None] * layers
    chunks = wires.seqs * wires.rows
    for n in reversed(range(layers)):
        norm_rows = norm_params[n]
        x_full, o_own, o_other, saved, probs, resid, gathered, pre_norm = kept[n]
        d_pre, d_gain_two, d_bias_two = norm_back(pre_norm, norm_rows[2], norm_rows[3], d_stream)
        d_middle, grad_in, grad_down = ffn_backward(d_pre.astype(BF), gathered, ffn_in[n], ffn_out[n])
        d_resid, d_gain_one, d_bias_one = norm_back(resid, norm_rows[0], norm_rows[1], d_pre + d_middle)
        d_branch = d_resid.astype(BF)
        d_branch_full = wires.in_order(d_branch, wires.core_swap(d_branch), 0)
        d_qkv, d_ext, d_x = attn_bwd(d_branch_full, out_own[n], saved, probs, pe_bwd[n], rev, w_pairs[n])
        d_mine = lax.dynamic_slice_in_dim(d_x, core * local, local, 0)
        d_theirs = lax.dynamic_slice_in_dim(d_x, (1 - core) * local, local, 0)
        d_stream = d_resid + d_mine + wires.core_swap(d_theirs.astype(BF)).astype(F32)

        g_qkv = jnp.einsum("ld,plce->cdpe", x_full, d_qkv.reshape(pairs, length, 3, 128), preferred_element_type=F32)
        g_qkv = g_qkv.reshape(3, model, half)
        d_ext = (d_ext * SCALE).astype(BF)
        d_pq = jnp.einsum("peu,ub->peb", d_ext[:, 0], table, preferred_element_type=F32).astype(BF).reshape(half, -1)
        d_pk = jnp.einsum("peu,ub->peb", d_ext[:, 1], table[::-1], preferred_element_type=F32).astype(BF).reshape(half, -1)
        g_pos = jnp.stack([
            jnp.einsum("bd,eb->de", rel_table[n], d_pq, preferred_element_type=F32),
            jnp.einsum("bd,eb->de", rel_table[n], d_pk, preferred_element_type=F32),
        ])
        g_qkv = jnp.concatenate([g_qkv[:2] + g_pos, g_qkv[2:]], axis=0)
        g_rel = jnp.einsum("eb,de->bd", d_pq, qkv_own[n, 0], preferred_element_type=F32)
        g_rel = g_rel + jnp.einsum("eb,de->bd", d_pk, qkv_own[n, 1], preferred_element_type=F32)
        g_rel = own_blocks(g_rel, 1, core) + wires.core_swap(own_blocks(g_rel, 1, 1 - core).astype(BF)).astype(F32)
        d_cols = own_blocks(d_branch_full, 1, core)
        g_out_own = jnp.einsum("ld,le->de", o_own, d_cols, preferred_element_type=F32)
        g_out_other = jnp.einsum("ld,le->de", o_other, d_cols, preferred_element_type=F32)
        two = wires.cols // 2
        g_out = wires.in_order(
            g_out_own.reshape(two, 1, block, half), g_out_other.reshape(two, 1, block, half), 1
        ).reshape(model, half)
        def cut(array):
            lead = array.shape[:-2]
            count = array.shape[-2] // chunks
            array = array.astype(BF).reshape(lead + (chunks, count, two, block))
            nl = len(lead)
            array = jnp.moveaxis(array, (nl, nl + 2), (0, 1))
            return array.reshape(chunks, two, -1, block)

        packed = jnp.concatenate([cut(g_qkv), cut(g_out), cut(g_rel)], axis=2)
        packed = lax.psum_scatter(
            packed, "col", scatter_dimension=1, tiled=False,
            axis_index_groups=[[k, k + 2] for k in range(2)],
        )
        packed = lax.psum_scatter(packed, ("seq", "rows"), scatter_dimension=0, tiled=False).astype(F32)
        c1 = model // chunks
        q_part, o_part, r_part = packed[: 3 * c1], packed[3 * c1 : 4 * c1], packed[4 * c1 :]
        ffn = jnp.stack([grad_in, grad_down]).astype(BF)
        ffn = lax.psum_scatter(ffn, ("seq", "rows"), scatter_dimension=1, tiled=True).astype(F32)
        norms = jnp.stack([d_gain_one, d_bias_one, d_gain_two, d_bias_two])
        grads[n] = (q_part.reshape(3, c1, block), o_part, r_part, ffn[0], ffn[1], norms)
    d_input = wires.turn(d_stream)
    stacked = [jnp.stack([grads[n][k] for n in range(layers)]) for k in range(6)]
    norms = lax.psum(stacked[5], ("seq", "rows", "col"))
    norms = lax.dynamic_slice_in_dim(norms, wires.col, 1, 1)
    width = model // chunks
    norms = lax.dynamic_slice_in_dim(norms, (wires.seq * wires.rows + wires.row) * width, width, 2)
    return (output[None], d_input[None], stacked[0], stacked[1], stacked[2], stacked[3], stacked[4], norms)


def solution(mesh):
    placed = (
        P(("rows", "col"), "seq", None),
        P(("rows", "col"), None),
        P(),
        P(),
        P(),
        P(None, None, "col"),
        P(None, None, "col"),
        P(),
        P(("rows", "col"), "seq", None),
    )
    return jax.shard_map(
        per_device,
        mesh=mesh,
        in_specs=placed,
        out_specs=(
            P(("rows", "col"), "seq", None),
            P(("rows", "col"), "seq", None),
            P(None, None, ("seq", "rows"), "col"),
            P(None, ("seq", "rows"), "col"),
            P(None, ("seq", "rows"), "col"),
            P(None, ("seq", "rows"), "col"),
            P(None, ("seq", "rows"), "col"),
            P(None, "col", ("seq", "rows")),
        ),
        check_vma=False,
    )
```

time: 2260 us -> 875 us (0.39)
  local copies, waits for them, and re-layouts: 1270 us -> 155 us
  waiting for transfers between devices: 594 us -> 408 us
  matrix products: 264 us -> 89.8 us
  Pallas kernels: 0 us -> 82.6 us
    reshape x12 -> x13, local copies, waits for them, and re-layouts: 350 us -> 11.5 us  [the longest x4 7.43 us: cut(): array = array.astype(BF).reshape(lead + (chunks, count, two, block))]
    dynamic_update_slice x4 -> x0, local copies, waits for them, and re-layouts: 259 us -> none  [skew_rows(): part = lax.dynamic_slice_in_dim(flat, shift, count * (width - 1), len(lead))]
    unnamed x25 -> x14, waiting for transfers between devices: 257 us -> 0.23 us
    dynamic_slice x4 -> x5, local copies, waits for them, and re-layouts: 233 us -> 6.16 us  [the longest x4 5.51 us: own_blocks(): cut = lax.dynamic_index_in_dim(cut, which, axis + 1, keepdims=False)]
    unnamed x277 -> x159, local copies, waits for them, and re-layouts: 231 us -> 36.4 us
    dot_general x62 -> x37, matrix products: 264 us -> 89.8 us  [the longest x2 21.9 us: ffn_forward(): hidden = jnp.dot(gathered, w_in, preferred_element_type=F32)]
    pallas_call x0 -> x4, Pallas kernels: none -> 82.6 us  [the longest x2 44.2 us: attn_bwd(): pl.pallas_call(functools.partial(bwd_kernel, length=length, blk=128), out...]
    transpose x4 -> x2, local copies, waits for them, and re-layouts: 74.8 us -> 7.92 us  [cut(): array = jnp.moveaxis(array, (nl, nl + 2), (0, 1))]
  transfers between devices with their start and end apart: 20 -> 29, of which waited for: 15 -> 15; matrix products, arithmetic and copies ran while one was open for 36% -> 22% of each run, Pallas kernels for 0% -> 3%
where the time goes in v1:
time: 875 us; the launch traced here: 864 us
  waiting for transfers between devices  408 us (47%)
  local copies, waits for them, and re-layouts  155 us (18%)
  matrix products  89.8 us (10%)
  Pallas kernels  82.6 us (9%)
  other arithmetic  54.8 us (6%)
  blocking collectives  40.1 us (5%)
  starting transfers between devices  18.4 us (2%)
  between operations  15.5 us (2%)
    reduce_scatter x2, waiting for transfers between devices, per_device(): lax.psum_scatter(packed, ('seq', 'rows'), scatter_dimension=0, tiled=False)  133 us
    reduce_scatter x2, waiting for transfers between devices, per_device(): lax.psum_scatter(ffn, ('seq', 'rows'), scatter_dimension=1, tiled=True)  94.7 us
    reduce_scatter x2, waiting for transfers between devices, ffn_forward(): lax.psum_scatter(part, 'col', scatter_dimension=0, tiled=True).astype(F32)  52.1 us
    pallas_call x2, Pallas kernels, attn_bwd(): pl.pallas_call(functools.partial(bwd_kernel, length=length, blk=128), out...  44.2 us
    all_gather x2, waiting for transfers between devices, ffn_forward(): gathered = lax.all_gather(ffn_rows, 'col', axis=0, tiled=True)  40.8 us
    psum x1, blocking collectives, per_device(): norms = lax.psum(stacked[5], ('seq', 'rows', 'col'))  40.1 us
    all_gather x2, waiting for transfers between devices, ffn_backward(): cot_rows = lax.all_gather(d_rows, 'col', axis=0, tiled=True)  39.5 us
    pallas_call x2, Pallas kernels, attn_fwd(): pl.pallas_call(functools.partial(fwd_kernel, length=length, blk=128), out...  38.4 us
  transfers between devices with their start and end apart: 29, of which 15 were waited for; matrix products, arithmetic and copies ran while one was open for 22% of the time, Pallas kernels for 3%

profile of v1, /device:TPU:0, one launch (start us, length us, event | category | flops | bytes accessed | tf_op | source)
XLA Modules:
  0.0 864.2 jit_solution(7841934237149261448)
XLA Ops:
  8.5 4.5 collective-permute-start
  13.0 10.4 %copy.156 = bf16[2,3,768,768]{2,3,1,0:T(8,128)(2,1)} copy(bf16[2,3,768,768]{3,2,1,0:T(8,128)(2,1)} %param.13) | data formatting | bytes 14155776 | tf_op args[2]
  23.4 2.4 constant_dynamic-slice_fusion.9
  30.2 2.7 convolution_convert_fusion
  33.0 4.0 copy.158
  38.2 3.2 slice_bitcast_fusion.2
  43.7 19.2 %attention.2 = (bf16[512,384]{1,0:T(8,128)(2,1)}, bf16[3,512,384]{2,1,0:T(8,128)(2,1)S(1)}, bf16[6,512,512]{2,1,0:T(8,128)(2,1)}) custom-call(s32[4]{0:T(128)S(1)} %bitcast.284, bf16[512,768]{1,0:T(8,128)(2,1)S(1)} %pad_maximum_fusion.4.x_ref, bf16[3,768,384]{2,1,0:T(8,128)(2,1)S(1)} %copy.159.w_ref.wt_ref, ...), custom_call_target="tpu_custom_call" | custom-call | tf_op jit(solution)/shard_map/attention/pallas_call | solution.py:77
  70.4 21.4 %all-gather.5.cloned.1.call-done = bf16[1024,768]{1,0:T(8,128)(2,1)} async-done(((bf16[256,768]{1,0:T(8,128)(2,1)}), bf16[1024,768]{1,0:T(8,128)(2,1)}) %all-gather.5.cloned.1.call-update) | async-done | bytes 1572880 | tf_op jit(solution)/shard_map/all_gather | solution.py:250
  91.8 10.9 %fusion.2 = (bf16[1024,768]{1,0:T(8,128)(2,1)S(1)}, f32[1024,768]{1,0:T(8,128)}) fusion(bf16[1024,768]{1,0:T(8,128)(2,1)} %all-gather.5.cloned.1.call-done, bf16[2,768,768]{2,1,0:T(8,128)(2,1)} %param.16), kind=kOutput, calls=%fused_computation.8 | convolution fusion | flops 1259077632 | bytes 7471104 | tf_op jit(solution)/shard_map/dot_general | solution.py:251
  104.0 2.6 convolution_convert_fusion.5
  106.7 28.3 %reduce-scatter.11.cloned.1.call-done = bf16[256,768]{1,0:T(8,128)(2,1)} async-done(((bf16[1024,768]{1,0:T(8,128)(2,1)}), bf16[256,768]{1,0:T(8,128)(2,1)}) %reduce-scatter.11.cloned.1.call-update) | async-done | bytes 393232 | tf_op jit(solution)/shard_map/reduce_scatter | solution.py:254
  139.6 2.8 copy.162.w_ref.wt_ref
  145.5 19.3 %attention.3 = (bf16[512,384]{1,0:T(8,128)(2,1)S(1)}, bf16[3,512,384]{2,1,0:T(8,128)(2,1)S(1)}, bf16[6,512,512]{2,1,0:T(8,128)(2,1)}) custom-call(s32[4]{0:T(128)S(1)} %bitcast.285, bf16[512,768]{1,0:T(8,128)(2,1)S(1)} %pad_maximum_fusion.5.x_ref, bf16[3,768,384]{2,1,0:T(8,128)(2,1)S(1)} %copy.162.w_ref.wt_ref, bf16[3,2,640,128]{3,2,1,0:T(8,128)(2,1)S(1)} %copy-done.3, ...), custom_call_target="tpu_custom_call" | custom-call | tf_op jit(solution)/shard_map/attention/pallas_call | solution.py:77
  170.1 19.4 %all-gather.7.cloned.1.call-done = bf16[1024,768]{1,0:T(8,128)(2,1)} async-done(((bf16[256,768]{1,0:T(8,128)(2,1)}), bf16[1024,768]{1,0:T(8,128)(2,1)}) %all-gather.7.cloned.1.call-update) | async-done | bytes 1572880 | tf_op jit(solution)/shard_map/all_gather | solution.py:250
  189.5 10.9 %fusion.5 = (bf16[1024,768]{1,0:T(8,128)(2,1)S(1)}, f32[1024,768]{1,0:T(8,128)}) fusion(bf16[1024,768]{1,0:T(8,128)(2,1)} %all-gather.7.cloned.1.call-done, bf16[2,768,768]{2,1,0:T(8,128)(2,1)} %param.16), kind=kOutput, calls=%fused_computation.11 | convolution fusion | flops 1259077632 | bytes 7471104 | tf_op jit(solution)/shard_map/dot_general | solution.py:251
  201.6 2.7 convolution_convert_fusion.4
  204.3 4.5 collective-permute-start.7
  208.8 23.8 %reduce-scatter.13.cloned.1.call-done = bf16[256,768]{1,0:T(8,128)(2,1)} async-done(((bf16[1024,768]{1,0:T(8,128)(2,1)}), bf16[256,768]{1,0:T(8,128)(2,1)}) %reduce-scatter.13.cloned.1.call-update) | async-done | bytes 393232 | tf_op jit(solution)/shard_map/reduce_scatter | solution.py:254
  239.6 19.8 %all-gather.9.cloned.1.call-done = bf16[1024,768]{1,0:T(8,128)(2,1)} async-done(((bf16[256,768]{1,0:T(8,128)(2,1)}), bf16[1024,768]{1,0:T(8,128)(2,1)}) %all-gather.9.cloned.1.call-update) | async-done | bytes 1572880 | tf_op jit(solution)/shard_map/all_gather | solution.py:259
  259.4 4.8 fusion.11
  265.4 2.6 convolution_convert_fusion.3
  268.2 2.9 convolution_convert_fusion.10
  271.2 2.3 copy.164
  278.1 18.2 %reduce-scatter.15.cloned.1.call-done = bf16[256,768]{1,0:T(8,128)(2,1)} async-done(((bf16[1024,768]{1,0:T(8,128)(2,1)}), bf16[256,768]{1,0:T(8,128)(2,1)}) %reduce-scatter.15.cloned.1.call-update) | async-done | bytes 393232 | tf_op jit(solution)/shard_map/reduce_scatter | solution.py:266
  301.5 22.1 %attention_grad.2 = (bf16[3,512,384]{2,1,0:T(8,128)(2,1)S(1)}, f32[3,2,128,640]{3,2,1,0:T(8,128)}, f32[512,768]{1,0:T(8,128)}) custom-call(bf16[512,768]{1,0:T(8,128)(2,1)S(1)} %pad_maximum_fusion.6.drb_ref, bf16[384,768]{1,0:T(8,128)(2,1)S(1)} %bitcast.283, bf16[3,512,384]{2,1,0:T(8,128)(2,1)S(1)} %copy-done.7, ...), custom_call_target="tpu_custom_call" | custom-call | tf_op jit(solution)/shard_map/attention_grad/pallas_call | solution.py:169
  331.9 19.8 %all-gather.11.cloned.1.call-done = bf16[1024,768]{1,0:T(8,128)(2,1)} async-done(((bf16[256,768]{1,0:T(8,128)(2,1)}), bf16[1024,768]{1,0:T(8,128)(2,1)}) %all-gather.11.cloned.1.call-update) | async-done | bytes 1572880 | tf_op jit(solution)/shard_map/all_gather | solution.py:259
  351.6 4.8 fusion.17
  357.6 2.6 convolution_convert_fusion.2
  361.9 2.4 copy.179
  364.3 2.4 convolution_bitcast_fusion
  372.5 2.9 stack.99
  377.0 2.6 convolution_bitcast_fusion.3
  379.7 2.9 stack.98
  384.2 2.8 convolution_add_fusion
  387.0 3.0 copy.186
  392.2 3.4 copy.180
  396.4 4.4 slice.238
  400.8 3.2 fusion.19
  405.9 4.6 copy.181
  410.5 2.4 multiply_reduce_fusion.2
  419.2 2.4 copy.188
  430.5 3.5 pad_maximum_fusion.1
  434.0 5.9 copy.189
  441.2 22.2 %attention_grad.3 = (bf16[3,512,384]{2,1,0:T(8,128)(2,1)S(1)}, f32[3,2,128,640]{3,2,1,0:T(8,128)}, f32[512,768]{1,0:T(8,128)}) custom-call(bf16[512,768]{1,0:T(8,128)(2,1)S(1)} %pad_maximum_fusion.7.drb_ref, bf16[384,768]{1,0:T(8,128)(2,1)S(1)} %bitcast.281, bf16[3,512,384]{2,1,0:T(8,128)(2,1)S(1)} %copy-done.5, ...), custom_call_target="tpu_custom_call" | custom-call | tf_op jit(solution)/shard_map/attention_grad/pallas_call | solution.py:169
  464.5 2.4 copy.167
  466.9 2.5 convolution_bitcast_fusion.1
  482.5 3.0 convolution_add_fusion.1
  485.5 3.0 copy.174
  492.2 3.4 slice.229
  498.6 2.9 fusion.18
  506.1 3.3 copy.169
  513.0 2.4 copy.176
  515.4 3.0 pad_maximum_fusion
  518.5 5.9 copy.177
  525.8 3.0 fusion.41
  532.7 3.0 fusion.39
  538.8 3.7 copy.190
  542.6 25.2 %reduce-scatter.19.cloned.1.call-done = bf16[8,1,448,192]{2,3,0,1:T(8,128)(2,1)} async-done(((bf16[8,2,448,192]{2,3,0,1:T(8,128)(2,1)}), bf16[8,1,448,192]{2,3,0,1:T(8,128)(2,1)}) %reduce-scatter.19.cloned.1.call-update) | async-done | bytes 1376272 | tf_op jit(solution)/shard_map/reduce_scatter | solution.py:364
  567.9 3.7 copy.178
  576.5 64.7 %reduce-scatter.29.cloned.1.call-done = bf16[2,96,768]{2,1,0:T(8,128)(2,1)} async-done(((bf16[2,768,768]{2,1,0:T(8,128)(2,1)}), bf16[2,96,768]{2,1,0:T(8,128)(2,1)}) %reduce-scatter.29.cloned.1.call-update) | async-done | bytes 294928 | tf_op jit(solution)/shard_map/reduce_scatter | solution.py:372
  642.3 40.1 %psum.7 = f32[2,4,768]{2,1,0:T(4,128)S(1)} all-reduce(f32[2,4,768]{2,1,0:T(4,128)S(1)} %pad_maximum_fusion.15), channel_id=1, replica_groups=mesh['seq'=2,'rows'=4,'col'=4] {'seq','rows','col'}, use_global_device_ids=true, to_apply=%region_35.36 | all-reduce | flops 6144 | bytes 49152 | tf_op jit(solution)/shard_map/psum | solution.py:377
  683.1 30.0 %reduce-scatter.27.cloned.1.call-done = bf16[2,96,768]{2,1,0:T(8,128)(2,1)} async-done(((bf16[2,768,768]{2,1,0:T(8,128)(2,1)}), bf16[2,96,768]{2,1,0:T(8,128)(2,1)}) %reduce-scatter.27.cloned.1.call-update) | async-done | bytes 294928 | tf_op jit(solution)/shard_map/reduce_scatter | solution.py:372
  715.2 66.6 %reduce-scatter.25.cloned.1.call-done = bf16[1,448,192]{2,1,0:T(8,128)(2,1)} async-done(((bf16[8,448,192]{2,1,0:T(8,128)(2,1)}), bf16[1,448,192]{2,1,0:T(8,128)(2,1)}) %reduce-scatter.25.cloned.1.call-update) | async-done | bytes 172048 | tf_op jit(solution)/shard_map/reduce_scatter | solution.py:368
  784.3 66.6 %reduce-scatter.21.cloned.1.call-done = bf16[1,448,192]{2,1,0:T(8,128)(2,1)} async-done(((bf16[8,448,192]{2,1,0:T(8,128)(2,1)}), bf16[1,448,192]{2,1,0:T(8,128)(2,1)}) %reduce-scatter.21.cloned.1.call-update) | async-done | bytes 172048 | tf_op jit(solution)/shard_map/reduce_scatter | solution.py:368
  (350 shorter events, 146.6 us)
Async XLA Ops:
  7.2 84.6 %all-gather.5.cloned.1.call-start = ((), (), s32[]{:S(2)}) async-start(), calls=%async_computation.10 | async-start | bytes 1966080 | tf_op jit(solution)/shard_map/all_gather | solution.py:250
  7.2 34.2 %collective-permute-start.1 = (s32[1,4]{1,0:T(1,128)}, s32[1,4]{1,0:T(1,128)S(1)}, u32[]{:S(2)}, u32[]{:S(2)}) collective-permute-start(s32[1,4]{1,0:T(1,128)} %param.12), channel_id=1, source_target_pairs={{0,0},{1,16},{2,2},{3,18},{4,4},{5,20},{6,6},{7,22},{8,8},{9,24},{... | collective-permute-start | bytes 56 | tf_op jit(solution)/shard_map/ppermute | solution.py:235
  8.5 20.6 %collective-permute-start = (bf16[256,768]{1,0:T(8,128)(2,1)}, bf16[256,768]{1,0:T(8,128)(2,1)}, u32[]{:S(2)}, u32[]{:S(2)}) collective-permute-start(bf16[256,768]{1,0:T(8,128)(2,1)} %bitcast.339), channel_id=1, source_target_pairs={{0,0},{1,16},{2,2},{3,18},{4,4},{5,20},{6,6},{7,22},{8,8},{9,24},{... | collective-permute-start | bytes 1179656 | tf_op jit(solution)/shard_map/ppermute | solution.py:235
  29.1 12.6 %collective-permute-start.2 = (bf16[256,768]{1,0:T(8,128)(2,1)}, bf16[256,768]{1,0:T(8,128)(2,1)}, u32[]{:S(2)}, u32[]{:S(2)}) collective-permute-start(bf16[256,768]{1,0:T(8,128)(2,1)} %collective-permute-done), channel_id=1, source_target_pairs={{0,1},{1,0},{2,3},{3,2},{4,5},{5,4},{6,7},{7,6},{8,9},{9,8},{10,11... | collective-permute-start | bytes 1179656 | tf_op jit(solution)/shard_map/ppermute | solution.py:235
  38.2 5.5 copy-start
  38.2 5.5 copy-start.2
  42.8 21.1 %copy-start.40 = (bf16[2,768,768]{2,1,0:T(8,128)(2,1)S(1)}, bf16[2,768,768]{2,1,0:T(8,128)(2,1)}, u32[]{:S(2)}) copy-start(bf16[2,768,768]{2,1,0:T(8,128)(2,1)} %param.14) | copy-start | bytes 7077892
  63.9 2.6 collective-permute-start.3
  68.9 66.1 %copy-start.15 = (f32[256,768]{1,0:T(8,128)}, f32[256,768]{1,0:T(8,128)S(1)}, u32[]{:S(2)}) copy-start(f32[256,768]{1,0:T(8,128)S(1)} %get-tuple-element.101) | copy-start | bytes 2359300
  70.1 64.8 %reduce-scatter.11.cloned.1.call-start = ((), (), s32[]{:S(2)}) async-start(), calls=%async_computation.11 | async-start | bytes 1966080 | tf_op jit(solution)/shard_map/reduce_scatter | solution.py:254
  91.8 12.2 %copy-start.59 = (bf16[2,768,768]{2,1,0:T(8,128)(2,1)S(1)}, bf16[2,768,768]{2,1,0:T(8,128)(2,1)}, u32[]{:S(2)}) copy-start(bf16[2,768,768]{2,1,0:T(8,128)(2,1)} %param.17) | copy-start | bytes 7077892
  106.6 82.9 %all-gather.7.cloned.1.call-start = ((), (), s32[]{:S(2)}) async-start(), calls=%async_computation.12 | async-start | bytes 1966080 | tf_op jit(solution)/shard_map/all_gather | solution.py:250
  135.0 3.3 copy-start.25
  138.3 4.1 collective-permute-start.4
  142.4 22.4 %copy-start.1 = (bf16[3,768,384]{2,1,0:T(8,128)(2,1)}, bf16[3,768,384]{2,1,0:T(8,128)(2,1)S(1)}, u32[]{:S(2)}) copy-start(bf16[3,768,384]{2,1,0:T(8,128)(2,1)S(1)} %copy.162.w_ref.wt_ref) | copy-start | bytes 5308420
  145.5 22.2 %copy-start.13 = (f32[256,768]{1,0:T(8,128)S(1)}, f32[256,768]{1,0:T(8,128)}, u32[]{:S(2)}) copy-start(f32[256,768]{1,0:T(8,128)} %copy-done.12) | copy-start | bytes 2359300
  145.5 22.2 %copy-start.41 = (bf16[1,2,1,192,768]{4,3,2,1,0:T(8,128)(2,1)S(1)}, bf16[1,2,1,192,768]{4,3,2,1,0:T(8,128)(2,1)}, u32[]{:S(2)}) copy-start(bf16[1,2,1,192,768]{4,3,2,1,0:T(8,128)(2,1)} %get-tuple-element.75) | copy-start | bytes 1769476
  165.8 1.8 collective-permute-start.5
  169.6 62.9 %reduce-scatter.13.cloned.1.call-start = ((), (), s32[]{:S(2)}) async-start(), calls=%async_computation.13 | async-start | bytes 1966080 | tf_op jit(solution)/shard_map/reduce_scatter | solution.py:254
  189.5 12.1 %copy-start.60 = (bf16[2,768,768]{2,1,0:T(8,128)(2,1)S(1)}, bf16[2,768,768]{2,1,0:T(8,128)(2,1)}, u32[]{:S(2)}) copy-start(bf16[2,768,768]{2,1,0:T(8,128)(2,1)} %param.17) | copy-start | bytes 7077892
  204.3 55.1 %all-gather.9.cloned.1.call-start = ((), (), s32[]{:S(2)}) async-start(), calls=%async_computation.14 | async-start | bytes 1966080 | tf_op jit(solution)/shard_map/all_gather | solution.py:259
  204.3 29.9 %collective-permute-start.7 = (bf16[256,768]{1,0:T(8,128)(2,1)}, bf16[256,768]{1,0:T(8,128)(2,1)}, u32[]{:S(2)}, u32[]{:S(2)}) collective-permute-start(bf16[256,768]{1,0:T(8,128)(2,1)} %bitcast.30), channel_id=1, source_target_pairs={{0,0},{1,16},{2,2},{3,18},{4,4},{5,20},{6,6},{7,22},{8,8},{9,24},{... | collective-permute-start | bytes 1179656 | tf_op jit(solution)/shard_map/ppermute | solution.py:235
  239.5 56.8 %reduce-scatter.15.cloned.1.call-start = ((), (), s32[]{:S(2)}) async-start(), calls=%async_computation.15 | async-start | bytes 1966080 | tf_op jit(solution)/shard_map/reduce_scatter | solution.py:266
  259.4 6.0 copy-start.61
  268.0 83.6 %all-gather.11.cloned.1.call-start = ((), (), s32[]{:S(2)}) async-start(), calls=%async_computation.16 | async-start | bytes 1966080 | tf_op jit(solution)/shard_map/all_gather | solution.py:259
  271.2 25.1 %copy-start.23 = (f32[256,768]{1,0:T(8,128)S(1)}, f32[256,768]{1,0:T(8,128)}, u32[]{:S(2)}) copy-start(f32[256,768]{1,0:T(8,128)} %copy-done.22) | copy-start | bytes 2359300
  299.5 1.8 collective-permute-start.8
  301.5 26.0 %copy-start.14 = (f32[256,768]{1,0:T(8,128)S(1)}, f32[256,768]{1,0:T(8,128)}, u32[]{:S(2)}) copy-start(f32[256,768]{1,0:T(8,128)} %copy-done.12) | copy-start | bytes 2359300
  325.7 1.8 collective-permute-start.9
  331.8 78.7 %reduce-scatter.17.cloned.1.call-start = ((), (), s32[]{:S(2)}) async-start(), calls=%async_computation.17 | async-start | bytes 1966080 | tf_op jit(solution)/shard_map/reduce_scatter | solution.py:266
  351.6 6.0 copy-start.62
  360.2 4.1 copy-start.36
  360.2 178.6 %reduce-scatter.23.cloned.1.call-start = ((), (), s32[]{:S(2)}) async-start(), calls=%async_computation.20 | async-start | bytes 4718592 | tf_op jit(solution)/shard_map/reduce_scatter | solution.py:364
  366.8 3.7 copy-start.68
  392.0 24.8 %collective-permute-start.14 = (bf16[512,384]{0,1:T(8,128)(2,1)}, bf16[512,384]{0,1:T(8,128)(2,1)}, u32[]{:S(2)}, u32[]{:S(2)}) collective-permute-start(bf16[512,384]{0,1:T(8,128)(2,1)} %bitcast.93), channel_id=1, source_target_pairs={{0,1},{1,0},{2,3},{3,2},{4,5},{5,4},{6,7},{7,6},{8,9},{9,8},{10,11... | collective-permute-start | bytes 1179656 | tf_op jit(solution)/shard_map/ppermute | solution.py:235
  405.9 4.6 copy-start.16
  410.5 6.2 copy-start.32
  414.7 6.9 copy-start.55
  416.4 5.2 copy-start.19
  416.4 5.2 collective-permute-start.10
  421.6 4.4 copy-start.11
  439.9 128.0 %reduce-scatter.19.cloned.1.call-start = ((), (), s32[]{:S(2)}) async-start(), calls=%async_computation.18 | async-start | bytes 4718592 | tf_op jit(solution)/shard_map/reduce_scatter | solution.py:364
  470.3 4.1 copy-start.28
  474.4 4.0 copy-start.29
  478.9 3.6 copy-start.46
  482.4 8.2 slice-start
  490.4 20.1 %collective-permute-start.13 = (bf16[512,384]{0,1:T(8,128)(2,1)}, bf16[512,384]{0,1:T(8,128)(2,1)}, u32[]{:S(2)}, u32[]{:S(2)}) collective-permute-start(bf16[512,384]{0,1:T(8,128)(2,1)} %bitcast.65), channel_id=1, source_target_pairs={{0,1},{1,0},{2,3},{3,2},{4,5},{5,4},{6,7},{7,6},{8,9},{9,8},{10,11... | collective-permute-start | bytes 1179656 | tf_op jit(solution)/shard_map/ppermute | solution.py:235
  492.2 3.4 copy-start.44
  524.4 4.4 copy-start.64
  524.4 116.8 %reduce-scatter.29.cloned.1.call-start = ((), (), s32[]{:S(2)}) async-start(), calls=%async_computation.23 | async-start | bytes 2654208 | tf_op jit(solution)/shard_map/reduce_scatter | solution.py:372
  531.9 3.7 copy-start.63
  531.9 181.1 %reduce-scatter.27.cloned.1.call-start = ((), (), s32[]{:S(2)}) async-start(), calls=%async_computation.22 | async-start | bytes 2654208 | tf_op jit(solution)/shard_map/reduce_scatter | solution.py:372
  538.8 243.0 %reduce-scatter.25.cloned.1.call-start = ((), (), s32[]{:S(2)}) async-start(), calls=%async_computation.21 | async-start | bytes 2064384 | tf_op jit(solution)/shard_map/reduce_scatter | solution.py:368
  542.5 29.1 %copy-start.49 = (f32[512,768]{1,0:T(8,128)S(1)}, f32[512,768]{1,0:T(8,128)}, u32[]{:S(2)}) copy-start(f32[512,768]{1,0:T(8,128)} %get-tuple-element.27) | copy-start | bytes 4718596
  542.5 31.0 %copy-start.20 = (f32[256,768]{1,0:T(8,128)S(1)}, f32[256,768]{1,0:T(8,128)}, u32[]{:S(2)}) copy-start(f32[256,768]{1,0:T(8,128)} %copy-done.18) | copy-start | bytes 2359300
  542.6 31.0 %copy-start.56 = (f32[256]{0:T(256)S(1)}, f32[256]{0:T(256)}, u32[]{:S(2)}) copy-start(f32[256]{0:T(256)} %copy-done.55) | copy-start | bytes 3076
  542.6 308.3 %reduce-scatter.21.cloned.1.call-start = ((), (), s32[]{:S(2)}) async-start(), calls=%async_computation.19 | async-start | bytes 2064384 | tf_op jit(solution)/shard_map/reduce_scatter | solution.py:368
  571.6 4.9 copy-start.58
  571.6 4.9 copy-start.57
  571.6 70.7 %copy-start.54 = (f32[768]{0:T(1024)S(1)}, f32[768]{0:T(1024)}, u32[]{:S(2)}) copy-start(f32[768]{0:T(1024)} %get-tuple-element.40) | copy-start | bytes 9220
  571.6 70.7 %copy-start.53 = (f32[768]{0:T(1024)S(1)}, f32[768]{0:T(1024)}, u32[]{:S(2)}) copy-start(f32[768]{0:T(1024)} %get-tuple-element.46) | copy-start | bytes 9220
  571.7 1.9 collective-permute-start.11
  571.7 4.7 collective-permute-start.6
  574.6 108.5 %collective-permute-start.12 = (f32[256,768]{1,0:T(8,128)}, f32[256,768]{1,0:T(8,128)S(1)}, u32[]{:S(2)}, u32[]{:S(2)}) collective-permute-start(f32[256,768]{1,0:T(8,128)} %convert_add_fusion), channel_id=1, source_target_pairs={{0,0},{1,16},{2,2},{3,18},{4,4},{5,20},{6,6},{7,22},{8,8},{9,24},{... | collective-permute-start | bytes 2359304 | tf_op jit(solution)/shard_map/ppermute | solution.py:235
  (44 other events, 76.3 us)
Sparse Core Ops, SparseCore 0:
  70.3 21.4 all-gather.4
  106.8 28.1 reduce-scatter.10
  169.8 19.6 all-gather.6
  204.4 28.1 reduce-scatter.12
  239.7 19.6 all-gather.8
  268.1 28.1 reduce-scatter.14
  331.9 19.6 all-gather.10
  360.4 28.1 reduce-scatter.16
  440.0 43.3 reduce-scatter.22
  524.5 43.3 reduce-scatter.18
  571.4 69.7 reduce-scatter.28
  644.5 68.4 reduce-scatter.26
  716.5 65.1 reduce-scatter.24
  785.5 65.3 reduce-scatter.20
